TPU v7x, 128 devices: a whole 4x4x4 slice. The times are simulated.
128 devices in a mesh: rep: 4 (over y_lo, core), fsdp: 32 (over z, x, y_hi).
Axes of the slice: x: 4, y: 4 (y_hi: 2, y_lo: 2; y = y_hi * 2 + y_lo), z: 4, core: 2. Of those that a mesh axis runs over, the one named last changes fastest.
Arguments:
- acts: bfloat16 [98304, 8192], P(('rep', 'fsdp')), may hold values from -24 to 24
- cots: bfloat16 [98304, 1024], P(('rep', 'fsdp')), may hold values from -0.038085938 to 0.038085938
- inner_w: float32 [4, 8192, 1024], P('rep', 'fsdp'), may hold values from -6 to 6
- first_moment: float32 [4, 8192, 1024], P('rep', 'fsdp'), may hold values from -6 to 6
- second_moment: float32 [4, 8192, 1024], P('rep', 'fsdp'), may hold values from 0.05 to 2
- anchor: float32 [8192, 1024], P('fsdp'), may hold values from -6 to 6
- momentum: float32 [8192, 1024], P('fsdp'), may hold values from -3 to 3
- fragment: int32 [1], replicated, may hold values from 0 to 7
Outputs:
- new_w: float32 [4, 8192, 1024], P('rep', 'fsdp')
- new_first: float32 [4, 8192, 1024], P('rep', 'fsdp')
- new_second: float32 [4, 8192, 1024], P('rep', 'fsdp')
- new_anchor: float32 [8192, 1024], P('fsdp')
- new_momentum: float32 [8192, 1024], P('fsdp')
Inputs may be any that keep to these rules, and one draw needn't show every extreme that they name: fragment k selects head k of the key projection for k < 4, else head k - 4 of the value projection.
All inputs are finite; a program needn't handle non-finite values.
Results may differ from a plain program's by a relative error of at most 0.0003.
Values may be sent and summed in bfloat16 or wider, within the bound.
No kernel may reach another device: no remote copies, remote signals or barrier semaphores. Data moves between devices by JAX's collectives and lax.ppermute only.
A program may use at most 192 MiB of HBM per device.

v0:
```python
import jax
import jax.numpy as jnp
from jax import lax
from jax.sharding import PartitionSpec as P

HEAD_DIM = 128
INNER_STEP = 100


beta_first = 0.9
beta_second = 0.95
epsilon = 1e-08
inner_rate = 0.00015
decay_rate = 0.1
outer_rate = 0.7
outer_factor = 0.9
mixing_share = 0.5


def per_device(acts, cots, inner_w, first_moment, second_moment, anchor, momentum, fragment):
    span = HEAD_DIM
    grad = lax.psum_scatter(
        jnp.einsum("tk,tc->kc", acts, cots, preferred_element_type=jnp.float32),
        "fsdp",
        scatter_dimension=0,
        tiled=True,
    )
    weights = inner_w[0]
    new_first = beta_first * first_moment[0] + (1.0 - beta_first) * grad
    new_second = beta_second * second_moment[0] + (1.0 - beta_second) * grad * grad
    update = (
        new_first
        / (1.0 - beta_first**INNER_STEP)
        / (jnp.sqrt(new_second / (1.0 - beta_second**INNER_STEP)) + epsilon)
    )
    stepped = weights - inner_rate * (update + decay_rate * weights)
    column = fragment[0] * span
    groups = lax.axis_size("rep")
    drift = lax.dynamic_slice_in_dim(anchor, column, span, 1) - lax.dynamic_slice_in_dim(
        weights, column, span, 1
    )
    outer = lax.psum(drift, "rep") / groups
    momentum_part = outer_factor * lax.dynamic_slice_in_dim(momentum, column, span, 1) + outer
    anchor_next = lax.dynamic_slice_in_dim(anchor, column, span, 1) - outer_rate * (
        outer + outer_factor * momentum_part
    )
    new_momentum = lax.dynamic_update_slice_in_dim(momentum, momentum_part, column, 1)
    new_anchor = lax.dynamic_update_slice_in_dim(anchor, anchor_next, column, 1)
    mixed = (
        mixing_share * lax.dynamic_slice_in_dim(stepped, column, span, 1)
        + (1.0 - mixing_share) * anchor_next
    )
    new_w = lax.dynamic_update_slice_in_dim(stepped, mixed, column, 1)
    return (new_w[None], new_first[None], new_second[None], new_anchor, new_momentum)


def solution(mesh):
    placed = (
        P(("rep", "fsdp"), None),
        P(("rep", "fsdp"), None),
        P("rep", "fsdp", None),
        P("rep", "fsdp", None),
        P("rep", "fsdp", None),
        P("fsdp", None),
        P("fsdp", None),
        P(),
    )
    return jax.shard_map(
        per_device,
        mesh=mesh,
        in_specs=placed,
        out_specs=(
            P("rep", "fsdp", None),
            P("rep", "fsdp", None),
            P("rep", "fsdp", None),
            P("fsdp", None),
            P("fsdp", None),
        ),
        check_vma=False,
    )
```

profile of v0, /device:TPU:0, one launch (start us, length us, event | category | flops | bytes accessed | tf_op | source)
XLA Modules:
  0.0 765.0 jit_solution(17628670109000033765)
XLA Ops:
  8.0 0.0 copy-start
  8.0 0.0 reduce-scatter.2.cloned.1.call-start
  8.1 1.3 copy.20
  9.4 0.0 copy-start.1
  9.4 2.7 copy.21
  12.1 0.0 copy-done
  12.1 21.9 %fusion.6 = f32[8192,1024]{1,0:T(8,128)} fusion(bf16[768,8192]{1,0:T(8,128)(2,1)} %param.8, bf16[768,1024]{1,0:T(8,128)(2,1)S(1)} %copy-done), kind=kOutput, calls=%fused_computation.15 | convolution fusion | flops 12884901888 | bytes 47710208 | tf_op jit(solution)/shard_map/tk,tc->kc/dot_general | solution.py:23
  34.0 0.0 reduce-scatter.2.cloned.1.call-update
  34.0 0.0 all-reduce.2.cloned.1.call-start
  34.7 0.0 copy-done.1
  34.8 1.6 bitcast_subtract_fusion.1
  36.4 0.0 all-reduce.2.cloned.1.call-update
  36.4 712.4 %reduce-scatter.2.cloned.1.call-done = f32[256,1024]{1,0:T(8,128)} async-done(((f32[8192,1024]{1,0:T(8,128)}), f32[256,1024]{1,0:T(8,128)}) %reduce-scatter.2.cloned.1.call-update) | async-done | bytes 1048592 | tf_op jit(solution)/shard_map/reduce_scatter | solution.py:22
  748.7 4.3 fusion.4
  753.0 1.0 copy.14
  754.0 0.0 all-reduce.2.cloned.1.call-done
  754.0 1.7 bitcast_dynamic-update-slice_fusion
  755.8 1.8 fusion.5
Async XLA Ops:
  8.0 4.1 copy-start
  8.0 740.7 %reduce-scatter.2.cloned.1.call-start = ((), (), s32[]{:S(2)}) async-start(), calls=%async_computation.1 | async-start | bytes 34603008 | tf_op jit(solution)/shard_map/reduce_scatter | solution.py:22
  9.4 25.4 %copy-start.1 = (f32[256,1024]{1,0:T(8,128)}, f32[256,1024]{1,0:T(8,128)S(1)}, u32[]{:S(2)}) copy-start(f32[256,1024]{1,0:T(8,128)S(1)} %copy.20) | copy-start | bytes 3145732
  34.0 720.0 %all-reduce.2.cloned.1.call-start = ((), (), s32[]{:S(2)}) async-start(), calls=%async_computation.2 | async-start | bytes 262144 | tf_op jit(solution)/shard_map/psum | solution.py:42
Sparse Core Ops, SparseCore 0:
  34.2 714.5 reduce-scatter.1
Sparse Core Ops, SparseCore 1:
  37.0 142.5 all-reduce.1
where the time goes:
time: 766 us; the launch traced here: 765 us
  waiting for transfers between devices  712 us (93%)
  matrix products  21.9 us (3%)
  between operations  16.1 us (2%)
  other arithmetic  9.4 us (1%)
    reduce_scatter x1, waiting for transfers between devices, per_device(): lax.psum_scatter(jnp.einsum('tk,tc->kc', acts, cots, preferred_element_ty...  712 us
    dot_general x1, matrix products, per_device(): jnp.einsum('tk,tc->kc', acts, cots, preferred_element_type=jnp.float32)  21.9 us
  transfers between devices with their start and end apart: 2, of which 1 were waited for; matrix products, arithmetic and copies ran while one was open for 1% of the time, Pallas kernels for 0%

commit v1 on v0

v1 whole, which is shorter than its diff:
```python
import jax
import jax.numpy as jnp
from jax import lax
from jax.experimental import pallas as pl
from jax.experimental.pallas import tpu as pltpu
from jax.sharding import PartitionSpec as P

HEAD_DIM = 128
INNER_STEP = 100

beta_first = 0.9
beta_second = 0.95
epsilon = 1e-08
inner_rate = 0.00015
decay_rate = 0.1
outer_rate = 0.7
outer_factor = 0.9
mixing_share = 0.5

SENT = jnp.float16
WIDE, NARROW = 384, 256
RING = 4
TOK, ROWS = 768, 8192
BLOCK = 512


def wide(value):
    return value.astype(jnp.float32)


def tie(value, *others):
    return lax.optimization_barrier((value, *others))[0]


def dot_kernel(ids, acts, cots, out):
    out[...] = lax.dot_general(
        acts[...], cots[...], (((0,), (0,)), ((), ())), preferred_element_type=jnp.float32
    )


def dot_blocks(ids, acts, cots, part):
    count = ids.shape[0]
    return pl.pallas_call(
        dot_kernel,
        grid_spec=pltpu.PrefetchScalarGridSpec(
            num_scalar_prefetch=1,
            grid=(count,),
            in_specs=[
                pl.BlockSpec((TOK, BLOCK), lambda i, ids: (0, ids[i])),
                pl.BlockSpec((TOK, WIDE), lambda i, ids: (0, part)),
            ],
            out_specs=pl.BlockSpec((BLOCK, WIDE), lambda i, ids: (i, 0)),
        ),
        out_shape=jax.ShapeDtypeStruct((count * BLOCK, WIDE), jnp.float32),
        compiler_params=pltpu.CompilerParams(vmem_limit_bytes=16 << 20),
        cost_estimate=pl.CostEstimate(
            flops=2 * TOK * BLOCK * WIDE * count,
            bytes_accessed=2 * TOK * (BLOCK * count + WIDE) + 4 * BLOCK * WIDE * count,
            transcendentals=0,
        ),
        name="dot_blocks",
    )(ids, acts, cots)


def pair_kernel(ids, acts, cots, mine, other):
    full = lax.dot_general(
        acts[...], cots[...], (((0,), (0,)), ((), ())), preferred_element_type=jnp.float32
    )
    first = ids[0] == 0
    for k in range(full.shape[0] // 512):
        low, high = full[k * 512 : k * 512 + 256], full[k * 512 + 256 : k * 512 + 512]
        mine[k * 256 : k * 256 + 256] = jnp.where(first, low, high)
        other[k * 256 : k * 256 + 256] = jnp.where(first, high, low)


def dot_pairs(ids, acts, cots):
    block, count = 1024, ROWS // 1024
    shape = jax.ShapeDtypeStruct((ROWS // 2, NARROW), jnp.float32)
    return pl.pallas_call(
        pair_kernel,
        grid_spec=pltpu.PrefetchScalarGridSpec(
            num_scalar_prefetch=1,
            grid=(count,),
            in_specs=[
                pl.BlockSpec((TOK, block), lambda i, ids: (0, i)),
                pl.BlockSpec((TOK, NARROW), lambda i, ids: (0, 2 * WIDE // NARROW)),
            ],
            out_specs=[pl.BlockSpec((block // 2, NARROW), lambda i, ids: (i, 0))] * 2,
        ),
        out_shape=[shape, shape],
        compiler_params=pltpu.CompilerParams(vmem_limit_bytes=16 << 20),
        cost_estimate=pl.CostEstimate(
            flops=2 * TOK * ROWS * NARROW,
            bytes_accessed=2 * TOK * (ROWS + NARROW) + 4 * ROWS * NARROW,
            transcendentals=0,
        ),
        name="dot_pairs",
    )(ids, acts, cots)


AXES = ("rep", "fsdp")


def pairs_of(dz=0, dx=0, dh=0, dl=0, dc=0):
    place = lambda z, x, h, l, c: ((l * 2 + c) * RING + z) * RING * 2 + x * 2 + h
    return [
        (
            place(z, x, h, l, c),
            place((z + dz) % RING, (x + dx) % RING, (h + dh) % 2, (l + dl) % 2, (c + dc) % 2),
        )
        for z in range(RING)
        for x in range(RING)
        for h in range(2)
        for l in range(2)
        for c in range(2)
    ]


CHANNELS = {
    "z+": dict(dz=1),
    "z-": dict(dz=-1),
    "x+": dict(dx=1),
    "x-": dict(dx=-1),
    "y": dict(dh=1),
    "l": dict(dl=1),
    "c": dict(dc=1),
}


class Order:
    def __init__(self):
        self.arrived = {}
        self.last = None

    def after(self, value):
        return value if self.last is None else tie(value, self.last)

    def ran(self, value):
        self.last = value
        return value

    def send(self, value, step, channel=None):
        channel = channel or step
        if channel in self.arrived:
            value = tie(value, self.arrived[channel])
        got = lax.ppermute(value, AXES, pairs_of(**CHANNELS[step]))
        self.arrived[channel] = got
        return got


def split(value):
    return jnp.split(value, 2, 0)


def per_device(acts, cots, inner_w, first_moment, second_moment, anchor, momentum, fragment):
    span = HEAD_DIM
    me = lax.axis_index("fsdp")
    z, x, h = me // (2 * RING), (me // 2) % RING, me % 2
    order = Order()
    spots = jnp.arange(RING, dtype=jnp.int32)

    def dots(part, offset, where):
        if part == 0:
            ids = ((z + offset) % RING) * RING + spots[where]
        else:
            ids = spots[where] * RING + (x + offset) % RING
        return order.ran(dot_blocks(order.after(ids.astype(jnp.int32)), acts, cots, part))

    half0, half1, whole = slice(0, 2), slice(2, 4), slice(0, 4)

    first = {}
    for part, axis in ((0, "z"), (1, "x")):
        for half, way in ((half0, "+"), (half1, "-")):
            term = dots(part, 2, half).astype(SENT)
            first[axis + way] = order.send(order.ran(term), axis + way)
    mine_c, other_c = dot_pairs(order.after(h.reshape(1).astype(jnp.int32)), acts, cots)
    other_c = order.ran(other_c.astype(SENT))
    got_c = order.send(other_c, "y")

    second = {}
    for part, axis in ((0, "z"), (1, "x")):
        for way in "+-":
            term = dots(part, 1 if way == "+" else -1, whole)
            low, high = split(term)
            if way == "+":
                low = low + wide(first[axis + way])
            else:
                high = high + wide(first[axis + way])
            term = jnp.concatenate([low.astype(SENT), high.astype(SENT)], 0)
            second[axis + way] = order.send(order.ran(term), axis + way)
    own_a = dots(0, 0, whole)
    own_b = dots(1, 0, whole)

    sum_c = (mine_c + wide(got_c)).astype(SENT).reshape(RING, RING, 256, NARROW)
    sum_c = order.ran(order.after(sum_c))

    def at(array, position, axis=0):
        return lax.dynamic_index_in_dim(array, position % RING, axis, keepdims=False)

    def side(array):
        low, high = (jnp.concatenate([array[k], array[k + 1]], 1) for k in (0, 2))
        return jnp.concatenate([low, high], 0)

    c_z = lambda k: side(at(sum_c[..., :128], z + k, 0))
    c_x = lambda k: side(at(sum_c[..., 128:], x + k, 1))

    sum_a = order.ran(own_a + wide(second["z+"]) + wide(second["z-"])).astype(SENT)
    sum_b = order.ran(own_b + wide(second["x+"]) + wide(second["x-"])).astype(SENT)
    sum_a = sum_a.reshape(RING, BLOCK, WIDE)
    sum_b = sum_b.reshape(RING, BLOCK, WIDE)

    weights = inner_w[0]
    column = fragment[0] * span
    groups = lax.axis_size("rep")
    cut = lambda v: lax.dynamic_slice_in_dim(v, column, span, 1)
    drift = cut(anchor) - cut(weights)
    drift = drift + order.send(drift, "c", "y")
    drift = drift + order.send(drift, "l", "y")
    outer = drift / groups
    momentum_part = outer_factor * cut(momentum) + outer
    anchor_next = cut(anchor) - outer_rate * (outer + outer_factor * momentum_part)
    new_momentum = lax.dynamic_update_slice_in_dim(momentum, momentum_part, column, 1)
    new_anchor = lax.dynamic_update_slice_in_dim(anchor, anchor_next, column, 1)

    def both(axis):
        if axis == "z":
            return lambda k: jnp.concatenate([at(sum_b, z + k), c_z(k)], 1)
        return lambda k: jnp.concatenate([at(sum_a, x + k), c_x(k)], 1)

    def ring_sum(terms):
        near, mine = {}, {}
        for axis, term in terms.items():
            low, high = split(term(2))
            far_up = order.send(low, axis + "+")
            far_down = order.send(high, axis + "-")
            near[axis] = far_up, far_down
        for axis, term in terms.items():
            far_up, far_down = near[axis]
            low, high = split(term(1))
            up = jnp.concatenate([(wide(low) + wide(far_up)).astype(SENT), high], 0)
            up = order.send(up, axis + "+")
            low, high = split(term(-1))
            down = jnp.concatenate([low, (wide(high) + wide(far_down)).astype(SENT)], 0)
            down = order.send(down, axis + "-")
            mine[axis] = wide(term(0)) + wide(up) + wide(down)
        return mine

    quarter = ring_sum({"z": both("z"), "x": both("x")})
    sum_b, c1 = quarter["z"][:, :WIDE], quarter["z"][:, WIDE:]
    sum_a, c2 = quarter["x"][:, :WIDE], quarter["x"][:, WIDE:]

    pair = jnp.concatenate([sum_a, sum_b], 1).reshape(2, 256, 2 * WIDE)
    other = lax.dynamic_index_in_dim(pair, 1 - h, 0, keepdims=False).astype(SENT)
    mine = lax.dynamic_index_in_dim(pair, h, 0, keepdims=False)
    grad_ab = mine + wide(order.send(other, "y"))

    def back(array):
        return jnp.stack(
            [array[:256, :128], array[:256, 128:], array[256:, :128], array[256:, 128:]]
        ).astype(SENT)

    c1, c2 = back(c1), back(c2)
    final = ring_sum({"x": lambda k: at(c1, x + k), "z": lambda k: at(c2, z + k)})
    grad = jnp.concatenate([grad_ab, final["x"], final["z"]], 1)

    new_first = beta_first * first_moment[0] + (1.0 - beta_first) * grad
    new_second = beta_second * second_moment[0] + (1.0 - beta_second) * grad * grad
    update = (
        new_first
        / (1.0 - beta_first**INNER_STEP)
        / (jnp.sqrt(new_second / (1.0 - beta_second**INNER_STEP)) + epsilon)
    )
    stepped = weights - inner_rate * (update + decay_rate * weights)
    chosen = lax.broadcasted_iota(jnp.int32, stepped.shape, 1) // span == fragment[0]
    mixed = mixing_share * stepped + (1.0 - mixing_share) * new_anchor
    new_w = jnp.where(chosen, mixed, stepped)
    return (new_w[None], new_first[None], new_second[None], new_anchor, new_momentum)


def solution(mesh):
    placed = (
        P(("rep", "fsdp"), None),
        P(("rep", "fsdp"), None),
        P("rep", "fsdp", None),
        P("rep", "fsdp", None),
        P("rep", "fsdp", None),
        P("fsdp", None),
        P("fsdp", None),
        P(),
    )
    return jax.shard_map(
        per_device,
        mesh=mesh,
        in_specs=placed,
        out_specs=(
            P("rep", "fsdp", None),
            P("rep", "fsdp", None),
            P("rep", "fsdp", None),
            P("fsdp", None),
            P("fsdp", None),
        ),
        check_vma=False,
    )
```

time: 766 us -> 165 us (0.22)
  waiting for transfers between devices: 712 us -> 35.8 us
  starting transfers between devices: 0.08 us -> 42.8 us
  Pallas kernels: 0 us -> 34.4 us
  matrix products: 21.9 us -> 0 us
  other arithmetic: 9.4 us -> 30.1 us
  local copies, waits for them, and re-layouts: 5 us -> 19.8 us
  between operations: 16.1 us -> 2.08 us
    reduce_scatter x1 -> x0, waiting for transfers between devices: 712 us -> none  [per_device(): lax.psum_scatter(jnp.einsum('tk,tc->kc', acts, cots, preferred_element_ty...]
    ppermute x0 -> x28, starting transfers between devices: none -> 42.8 us  [send(): got = lax.ppermute(value, AXES, pairs_of(**CHANNELS[step]))]
    ppermute x0 -> x28, waiting for transfers between devices: none -> 35.8 us  [send(): got = lax.ppermute(value, AXES, pairs_of(**CHANNELS[step]))]
    pallas_call x0 -> x11, Pallas kernels: none -> 34.4 us  [the longest x10 28.1 us: dot_blocks(): pl.pallas_call(dot_kernel, grid_spec=pltpu.PrefetchScalarGridSpec(num_sca...]
    dot_general x1 -> x0, matrix products: 21.9 us -> none  [per_device(): jnp.einsum('tk,tc->kc', acts, cots, preferred_element_type=jnp.float32)]
    convert_element_type x0 -> x17, other arithmetic: none -> 16.3 us  [the longest x2 3.23 us: per_device(): term = jnp.concatenate([low.astype(SENT), high.astype(SENT)], 0)]
    unnamed x7 -> x35, local copies, waits for them, and re-layouts: 5 us -> 17.2 us
  transfers between devices with their start and end apart: 2 -> 28, of which waited for: 1 -> 11; matrix products, arithmetic and copies ran while one was open for 1% -> 17% of each run, Pallas kernels for 0% -> 20%
where the time goes in v1:
time: 165 us
  starting transfers between devices  42.8 us (26%)
  waiting for transfers between devices  35.8 us (22%)
  Pallas kernels  34.4 us (21%)
  other arithmetic  30.1 us (18%)
  local copies, waits for them, and re-layouts  19.8 us (12%)
  between operations  2.08 us (1%)
    ppermute x28, starting transfers between devices, send(): got = lax.ppermute(value, AXES, pairs_of(**CHANNELS[step]))  42.8 us
    ppermute x28, waiting for transfers between devices, send(): got = lax.ppermute(value, AXES, pairs_of(**CHANNELS[step]))  35.8 us
    pallas_call x10, Pallas kernels, dot_blocks(): pl.pallas_call(dot_kernel, grid_spec=pltpu.PrefetchScalarGridSpec(num_sca...  28.1 us
    unnamed x35, local copies, waits for them, and re-layouts  17.2 us
    pallas_call x1, Pallas kernels, dot_pairs(): pl.pallas_call(pair_kernel, grid_spec=pltpu.PrefetchScalarGridSpec(num_sc...  6.25 us
    another operation x4, other arithmetic  3.83 us
  transfers between devices with their start and end apart: 28, of which 11 were waited for; matrix products, arithmetic and copies ran while one was open for 17% of the time, Pallas kernels for 20%

profile of v1, /device:TPU:0, one launch (start us, length us, event | category | flops | bytes accessed | tf_op | source)
XLA Modules:
  0.0 165.0 jit_solution(2881622955978701471)
XLA Ops:
  3.3 4.6 %copy-done = bf16[768,8192]{1,0:T(8,128)(2,1)S(1)} copy-done((bf16[768,8192]{1,0:T(8,128)(2,1)S(1)}, bf16[768,8192]{1,0:T(8,128)(2,1)}, u32[]{:S(2)}) %copy-start) | copy-done | bytes 12582936
  7.8 2.0 %dot_blocks.10 = f32[1024,384]{1,0:T(8,128)S(1)} custom-call(s32[2]{0:T(128)S(1)} %get-tuple-element.159.ids, bf16[768,8192]{1,0:T(8,128)(2,1)S(1)} %copy-done, bf16[768,1024]{1,0:T(8,128)(2,1)S(1)} %copy-done.3), custom_call_target="tpu_custom_call" | custom-call | flops 603979776 | bytes 3735552 | tf_op jit(solution)/shard_map/dot_blocks/pallas_call | solution.py:43
  10.8 2.0 %collective-permute-start = (f16[1024,384]{1,0:T(8,128)(2,1)}, f16[1024,384]{1,0:T(8,128)(2,1)}, u32[]{:S(2)}, u32[]{:S(2)}) collective-permute-start(f16[1024,384]{1,0:T(8,128)(2,1)} %convert_element_type.204), channel_id=1, source_target_pairs={{0,8},{32,40},{64,72},{96,104},{1,9},{33,41},{65,73},{97,105},{2,1... | collective-permute-start | bytes 2359304 | tf_op jit(solution)/shard_map/ppermute | solution.py:146
  12.8 2.0 %dot_blocks.11 = f32[1024,384]{1,0:T(8,128)S(1)} custom-call(s32[2]{0:T(128)S(1)} %get-tuple-element.41.ids, bf16[768,8192]{1,0:T(8,128)(2,1)S(1)} %copy-done, bf16[768,1024]{1,0:T(8,128)(2,1)S(1)} %copy-done.3), custom_call_target="tpu_custom_call" | custom-call | flops 603979776 | bytes 3735552 | tf_op jit(solution)/shard_map/dot_blocks/pallas_call | solution.py:43
  15.8 2.1 %collective-permute-start.1 = (f16[1024,384]{1,0:T(8,128)(2,1)}, f16[1024,384]{1,0:T(8,128)(2,1)}, u32[]{:S(2)}, u32[]{:S(2)}) collective-permute-start(f16[1024,384]{1,0:T(8,128)(2,1)} %convert_element_type.205), channel_id=1, source_target_pairs={{0,24},{32,56},{64,88},{96,120},{1,25},{33,57},{65,89},{97,121},{2... | collective-permute-start | bytes 2359304 | tf_op jit(solution)/shard_map/ppermute | solution.py:146
  18.0 2.0 %dot_blocks.12 = f32[1024,384]{1,0:T(8,128)S(1)} custom-call(s32[2]{0:T(128)S(1)} %get-tuple-element.42.ids, bf16[768,8192]{1,0:T(8,128)(2,1)S(1)} %copy-done, bf16[768,1024]{1,0:T(8,128)(2,1)S(1)} %copy-done.3), custom_call_target="tpu_custom_call" | custom-call | flops 603979776 | bytes 3735552 | tf_op jit(solution)/shard_map/dot_blocks/pallas_call | solution.py:43
  21.0 1.5 collective-permute-start.2
  22.4 2.0 %dot_blocks.13 = f32[1024,384]{1,0:T(8,128)S(1)} custom-call(s32[2]{0:T(128)S(1)} %get-tuple-element.43.ids, bf16[768,8192]{1,0:T(8,128)(2,1)S(1)} %copy-done, bf16[768,1024]{1,0:T(8,128)(2,1)S(1)} %copy-done.3), custom_call_target="tpu_custom_call" | custom-call | flops 603979776 | bytes 3735552 | tf_op jit(solution)/shard_map/dot_blocks/pallas_call | solution.py:43
  24.6 1.8 %collective-permute-start.3 = (f16[1024,384]{1,0:T(8,128)(2,1)S(1)}, f16[1024,384]{1,0:T(8,128)(2,1)}, u32[]{:S(2)}, u32[]{:S(2)}) collective-permute-start(f16[1024,384]{1,0:T(8,128)(2,1)S(1)} %convert_element_type.207), channel_id=1, source_target_pairs={{0,6},{32,38},{64,70},{96,102},{1,7},{33,39},{65,71},{97,103},{2,0... | collective-permute-start | bytes 2359304 | tf_op jit(solution)/shard_map/ppermute | solution.py:146
  26.4 4.6 %copy-done.1 = bf16[768,8192]{1,0:T(8,128)(2,1)S(1)} copy-done((bf16[768,8192]{1,0:T(8,128)(2,1)S(1)}, bf16[768,8192]{1,0:T(8,128)(2,1)}, u32[]{:S(2)}) %copy-start.1) | copy-done | bytes 12582936
  31.0 6.3 %dot_pairs.1 = (f32[4096,256]{1,0:T(8,128)S(1)}, f32[4096,256]{1,0:T(8,128)S(1)}) custom-call(s32[1]{0:T(128)} %bitcast.3.ids, bf16[768,8192]{1,0:T(8,128)(2,1)S(1)} %copy-done.1, bf16[768,1024]{1,0:T(8,128)(2,1)S(1)} %copy-done.3), custom_call_target="tpu_custom_call" | custom-call | flops 3221225472 | bytes 21364736 | tf_op jit(solution)/shard_map/dot_pairs/pallas_call | solution.py:79
  37.2 1.9 %convert_element_type.208 = f16[4096,256]{1,0:T(8,128)(2,1)} convert(f32[4096,256]{1,0:T(8,128)S(1)} %get-tuple-element.45) | non-fusion elementwise | flops 1048576 | bytes 6291456 | tf_op jit(solution)/shard_map/convert_element_type | solution.py:177
  40.0 3.2 %collective-permute-start.6 = (f16[4096,256]{1,0:T(8,128)(2,1)}, f16[4096,256]{1,0:T(8,128)(2,1)}, u32[]{:S(2)}, u32[]{:S(2)}) collective-permute-start(f16[4096,256]{1,0:T(8,128)(2,1)} %convert_element_type.208), channel_id=1, source_target_pairs={{0,1},{32,33},{64,65},{96,97},{1,0},{33,32},{65,64},{97,96},{2,3},... | collective-permute-start | bytes 6291464 | tf_op jit(solution)/shard_map/ppermute | solution.py:146
  45.1 4.6 %copy-done.2 = bf16[768,8192]{1,0:T(8,128)(2,1)S(1)} copy-done((bf16[768,8192]{1,0:T(8,128)(2,1)S(1)}, bf16[768,8192]{1,0:T(8,128)(2,1)}, u32[]{:S(2)}) %copy-start.2) | copy-done | bytes 12582936
  49.7 3.4 %dot_blocks.14 = f32[2048,384]{1,0:T(8,128)S(1)} custom-call(s32[4]{0:T(128)S(1)} %iota_add_fusion.ids, bf16[768,8192]{1,0:T(8,128)(2,1)S(1)} %copy-done.2, bf16[768,1024]{1,0:T(8,128)(2,1)S(1)} %copy-done.3), custom_call_target="tpu_custom_call" | custom-call | flops 1207959552 | bytes 6881280 | tf_op jit(solution)/shard_map/dot_blocks/pallas_call | solution.py:43
  54.1 1.7 %fusion.3 = (f16[1024,384]{1,0:T(8,128)(2,1)S(1)}, f16[1024,384]{1,0:T(8,128)(2,1)S(1)}) fusion(f32[2048,384]{1,0:T(8,128)S(1)} %dot_blocks.14, f16[1024,384]{1,0:T(8,128)(2,1)} %collective-permute-done), kind=kLoop, calls=%fused_computation.14 | loop fusion | flops 1572864 | bytes 5505024 | tf_op jit(solution)/shard_map/convert_element_type | solution.py:189
  56.3 3.4 %dot_blocks.15 = f32[2048,384]{1,0:T(8,128)S(1)} custom-call(s32[4]{0:T(128)S(1)} %iota_add_fusion.1.ids, bf16[768,8192]{1,0:T(8,128)(2,1)S(1)} %bitcast.179, bf16[768,1024]{1,0:T(8,128)(2,1)S(1)} %copy-done.3), custom_call_target="tpu_custom_call" | custom-call | flops 1207959552 | bytes 6881280 | tf_op jit(solution)/shard_map/dot_blocks/pallas_call | solution.py:43
  59.7 1.5 slice_convert_fusion.2
  61.6 3.3 %collective-permute-start.5 = (f16[2048,384]{1,0:T(8,128)(2,1)S(1)}, f16[2048,384]{1,0:T(8,128)(2,1)}, u32[]{:S(2)}, u32[]{:S(2)}) collective-permute-start(f16[2048,384]{1,0:T(8,128)(2,1)S(1)} %pad_maximum_fusion.1), channel_id=1, source_target_pairs={{0,24},{32,56},{64,88},{96,120},{1,25},{33,57},{65,89},{97,121},{2... | collective-permute-start | bytes 4718600 | tf_op jit(solution)/shard_map/ppermute | solution.py:146
  64.9 3.4 %dot_blocks.16 = f32[2048,384]{1,0:T(8,128)S(1)} custom-call(s32[4]{0:T(128)S(1)} %fusion.24.ids, bf16[768,8192]{1,0:T(8,128)(2,1)S(1)} %bitcast.179, bf16[768,1024]{1,0:T(8,128)(2,1)S(1)} %copy-done.3), custom_call_target="tpu_custom_call" | custom-call | flops 1207959552 | bytes 6881280 | tf_op jit(solution)/shard_map/dot_blocks/pallas_call | solution.py:43
  68.3 1.5 fusion.1
  70.7 3.3 %dot_blocks.17 = f32[2048,384]{1,0:T(8,128)S(1)} custom-call(s32[4]{0:T(128)S(1)} %fusion.25.ids, bf16[768,8192]{1,0:T(8,128)(2,1)S(1)} %bitcast.179, bf16[768,1024]{1,0:T(8,128)(2,1)S(1)} %copy-done.3), custom_call_target="tpu_custom_call" | custom-call | flops 1207959552 | bytes 6881280 | tf_op jit(solution)/shard_map/dot_blocks/pallas_call | solution.py:43
  74.1 1.5 slice_convert_fusion
  76.0 3.0 %collective-permute-start.10 = (f16[2048,384]{1,0:T(8,128)(2,1)S(1)}, f16[2048,384]{1,0:T(8,128)(2,1)}, u32[]{:S(2)}, u32[]{:S(2)}) collective-permute-start(f16[2048,384]{1,0:T(8,128)(2,1)S(1)} %pad_maximum_fusion.3), channel_id=1, source_target_pairs={{0,6},{32,38},{64,70},{96,102},{1,7},{33,39},{65,71},{97,103},{2,0... | collective-permute-start | bytes 4718600 | tf_op jit(solution)/shard_map/ppermute | solution.py:146
  79.0 3.3 %dot_blocks.18 = f32[2048,384]{1,0:T(8,128)S(1)} custom-call(s32[4]{0:T(128)S(1)} %iota_add_fusion.2.ids, bf16[768,8192]{1,0:T(8,128)(2,1)S(1)} %bitcast.179, bf16[768,1024]{1,0:T(8,128)(2,1)S(1)} %copy-done.3), custom_call_target="tpu_custom_call" | custom-call | flops 1207959552 | bytes 6881280 | tf_op jit(solution)/shard_map/dot_blocks/pallas_call | solution.py:43
  82.4 3.4 %dot_blocks.19 = f32[2048,384]{1,0:T(8,128)S(1)} custom-call(s32[4]{0:T(128)S(1)} %fusion.23.ids, bf16[768,8192]{1,0:T(8,128)(2,1)S(1)} %bitcast.179, bf16[768,1024]{1,0:T(8,128)(2,1)S(1)} %copy-done.3), custom_call_target="tpu_custom_call" | custom-call | flops 1207959552 | bytes 6881280 | tf_op jit(solution)/shard_map/dot_blocks/pallas_call | solution.py:43
  85.8 2.6 %collective-permute-done.6 = f16[4096,256]{1,0:T(8,128)(2,1)} collective-permute-done((f16[4096,256]{1,0:T(8,128)(2,1)}, f16[4096,256]{1,0:T(8,128)(2,1)}, u32[]{:S(2)}, u32[]{:S(2)}) %collective-permute-start.6) | collective-permute-done | bytes 2097184 | tf_op jit(solution)/shard_map/ppermute | solution.py:146
  88.3 2.3 %add_convert_fusion = f16[4096,256]{1,0:T(8,128)(2,1)S(1)} fusion(f32[4096,256]{1,0:T(8,128)S(1)} %copy-done.5, f16[4096,256]{1,0:T(8,128)(2,1)} %collective-permute-done.6), kind=kLoop, calls=%fused_computation | loop fusion | flops 3145728 | bytes 8388608 | tf_op jit(solution)/shard_map/convert_element_type | solution.py:194
  91.8 1.6 collective-permute-start.18
  93.5 3.7 %collective-permute-done.5 = f16[2048,384]{1,0:T(8,128)(2,1)} collective-permute-done((f16[2048,384]{1,0:T(8,128)(2,1)S(1)}, f16[2048,384]{1,0:T(8,128)(2,1)}, u32[]{:S(2)}, u32[]{:S(2)}) %collective-permute-start.5) | collective-permute-done | bytes 1572896 | tf_op jit(solution)/shard_map/ppermute | solution.py:146
  97.1 2.6 %add_convert_fusion.2 = f16[2048,384]{1,0:T(8,128)(2,1)S(1)} fusion(f16[2048,384]{1,0:T(8,128)(2,1)} %collective-permute-done.5, f32[2048,384]{1,0:T(8,128)S(1)} %dot_blocks.18, f16[2048,384]{1,0:T(8,128)(2,1)} %collective-permute-done.4), kind=kLoop, calls=%fused_computation.2 | loop fusion | flops 3932160 | bytes 7864320 | tf_op jit(solution)/shard_map/convert_element_type | solution.py:207
  100.5 5.7 %collective-permute-done.7 = f16[2048,384]{1,0:T(8,128)(2,1)} collective-permute-done((f16[2048,384]{1,0:T(8,128)(2,1)S(1)}, f16[2048,384]{1,0:T(8,128)(2,1)}, u32[]{:S(2)}, u32[]{:S(2)}) %collective-permute-start.7) | collective-permute-done | bytes 1572896 | tf_op jit(solution)/shard_map/ppermute | solution.py:146
  106.2 4.5 %collective-permute-done.10 = f16[2048,384]{1,0:T(8,128)(2,1)} collective-permute-done((f16[2048,384]{1,0:T(8,128)(2,1)S(1)}, f16[2048,384]{1,0:T(8,128)(2,1)}, u32[]{:S(2)}, u32[]{:S(2)}) %collective-permute-start.10) | collective-permute-done | bytes 1572896 | tf_op jit(solution)/shard_map/ppermute | solution.py:146
  110.7 3.8 %collective-permute-start.11 = (f16[256,640]{1,0:T(8,128)(2,1)S(1)}, f16[256,640]{1,0:T(8,128)(2,1)S(1)}, u32[]{:S(2)}, u32[]{:S(2)}) collective-permute-start(f16[256,640]{1,0:T(8,128)(2,1)S(1)} %get-tuple-element.60), channel_id=1, source_target_pairs={{0,6},{32,38},{64,70},{96,102},{1,7},{33,39},{65,71},{97,103},{2,0... | collective-permute-start | bytes 983048 | tf_op jit(solution)/shard_map/ppermute | solution.py:146
  114.5 2.6 %add_convert_fusion.1 = f16[2048,384]{1,0:T(8,128)(2,1)S(1)} fusion(f16[2048,384]{1,0:T(8,128)(2,1)} %collective-permute-done.10, f32[2048,384]{1,0:T(8,128)S(1)} %dot_blocks.19, f16[2048,384]{1,0:T(8,128)(2,1)} %collective-permute-done.7), kind=kLoop, calls=%fused_computation.1 | loop fusion | flops 3932160 | bytes 7864320 | tf_op jit(solution)/shard_map/convert_element_type | solution.py:208
  121.5 1.5 collective-permute-done.8
  123.4 3.2 %collective-permute-start.12 = (f16[512,640]{1,0:T(8,128)(2,1)S(1)}, f16[512,640]{1,0:T(8,128)(2,1)S(1)}, u32[]{:S(2)}, u32[]{:S(2)}) collective-permute-start(f16[512,640]{1,0:T(8,128)(2,1)S(1)} %pad_maximum_fusion.8), channel_id=1, source_target_pairs={{0,6},{32,38},{64,70},{96,102},{1,7},{33,39},{65,71},{97,103},{2,0... | collective-permute-start | bytes 1966088 | tf_op jit(solution)/shard_map/ppermute | solution.py:146
  126.9 1.6 collective-permute-done.13
  130.0 2.1 %collective-permute-start.16 = (f16[512,640]{1,0:T(8,128)(2,1)S(1)}, f16[512,640]{1,0:T(8,128)(2,1)S(1)}, u32[]{:S(2)}, u32[]{:S(2)}) collective-permute-start(f16[512,640]{1,0:T(8,128)(2,1)S(1)} %pad_maximum_fusion.10), channel_id=1, source_target_pairs={{0,24},{32,56},{64,88},{96,120},{1,25},{33,57},{65,89},{97,121},{2... | collective-permute-start | bytes 1966088 | tf_op jit(solution)/shard_map/ppermute | solution.py:146
  132.1 4.8 %collective-permute-done.9 = f16[512,640]{1,0:T(8,128)(2,1)S(1)} collective-permute-done((f16[512,640]{1,0:T(8,128)(2,1)S(1)}, f16[512,640]{1,0:T(8,128)(2,1)S(1)}, u32[]{:S(2)}, u32[]{:S(2)}) %collective-permute-start.9) | collective-permute-done | bytes 655392 | tf_op jit(solution)/shard_map/ppermute | solution.py:146
  137.5 4.8 %collective-permute-done.14 = f16[512,640]{1,0:T(8,128)(2,1)S(1)} collective-permute-done((f16[512,640]{1,0:T(8,128)(2,1)S(1)}, f16[512,640]{1,0:T(8,128)(2,1)S(1)}, u32[]{:S(2)}, u32[]{:S(2)}) %collective-permute-start.14) | collective-permute-done | bytes 655392 | tf_op jit(solution)/shard_map/ppermute | solution.py:146
  142.6 3.0 %collective-permute-start.26 = (f16[128,128]{1,0:T(8,128)(2,1)S(1)}, f16[128,128]{1,0:T(8,128)(2,1)S(1)}, u32[]{:S(2)}, u32[]{:S(2)}) collective-permute-start(f16[128,128]{1,0:T(8,128)(2,1)S(1)} %get-tuple-element.75), channel_id=1, source_target_pairs={{0,24},{32,56},{64,88},{96,120},{1,25},{33,57},{65,89},{97,121},{2... | collective-permute-start | bytes 98312 | tf_op jit(solution)/shard_map/ppermute | solution.py:146
  146.2 3.3 %collective-permute-start.22 = (f16[128,128]{1,0:T(8,128)(2,1)S(1)}, f16[128,128]{1,0:T(8,128)(2,1)S(1)}, u32[]{:S(2)}, u32[]{:S(2)}) collective-permute-start(f16[128,128]{1,0:T(8,128)(2,1)S(1)} %get-tuple-element.71), channel_id=1, source_target_pairs={{0,6},{32,38},{64,70},{96,102},{1,7},{33,39},{65,71},{97,103},{2,0... | collective-permute-start | bytes 98312 | tf_op jit(solution)/shard_map/ppermute | solution.py:146
  152.4 2.3 %collective-permute-done.20 = f16[128,128]{1,0:T(8,128)(2,1)S(1)} collective-permute-done((f16[128,128]{1,0:T(8,128)(2,1)S(1)}, f16[128,128]{1,0:T(8,128)(2,1)S(1)}, u32[]{:S(2)}, u32[]{:S(2)}) %collective-permute-start.20) | collective-permute-done | bytes 32800 | tf_op jit(solution)/shard_map/ppermute | solution.py:146
  156.8 2.2 %collective-permute-done.23 = f16[256,128]{1,0:T(8,128)(2,1)S(1)} collective-permute-done((f16[256,128]{1,0:T(8,128)(2,1)S(1)}, f16[256,128]{1,0:T(8,128)(2,1)S(1)}, u32[]{:S(2)}, u32[]{:S(2)}) %collective-permute-start.23) | collective-permute-done | bytes 65568 | tf_op jit(solution)/shard_map/ppermute | solution.py:146
  159.0 2.2 %collective-permute-done.21 = f16[256,128]{1,0:T(8,128)(2,1)S(1)} collective-permute-done((f16[256,128]{1,0:T(8,128)(2,1)S(1)}, f16[256,128]{1,0:T(8,128)(2,1)S(1)}, u32[]{:S(2)}, u32[]{:S(2)}) %collective-permute-start.21) | collective-permute-done | bytes 65568 | tf_op jit(solution)/shard_map/ppermute | solution.py:146
  161.5 1.7 %fusion.10 = (f32[1,256,1024]{2,1,0:T(8,128)}, f32[1,256,1024]{2,1,0:T(8,128)}) fusion(f32[1,256,1024]{2,1,0:T(8,128)S(1)} %copy-done.7, f32[1,256,128]{2,1,0:T(8,128)S(1)} %bitcast.186, f32[1,256,128]{2,1,0:T(8,128)S(1)} %bitcast.187, f32[1,256,768]{2,1,0:T(8,128)S(1)} %bitcast.181, f32[1,256,1024]{2,1,0:T(8,128)S(1)} %copy-done.8), kind=kLoop, calls=%fused_computation.30 | loop fusion | flops 2359296 | bytes 5242880 | tf_op jit(solution)/shard_map/add | solution.py:267
  163.1 1.9 %select_bitcast_fusion = f32[1,256,1024]{2,1,0:T(8,128)} fusion(f32[256,1024]{1,0:T(8,128)S(1)} %get-tuple-element.100, f32[1,256,1024]{2,1,0:T(8,128)S(1)} %copy-done.11, f32[256,128]{1,0:T(8,128)S(1)} %fusion.13, f32[256,128]{1,0:T(8,128)S(1)} %fusion.14, f32[256,768]{1,0:T(8,128)S(1)} %bitcast_add_fusion.1, f32[1,256,1024]{2,1,0:T(8,128)S(1)} %copy-done.7, ...), kind=kLoop, calls=%fused_computation.38 | loop fusion | flops 5767168 | bytes 6300676 | tf_op jit(solution)/shard_map/broadcast_in_dim | solution.py:277
  (133 shorter events, 25.9 us)
Async XLA Ops:
  1.9 1.4 copy-start.3
  3.3 4.6 %copy-start = (bf16[768,8192]{1,0:T(8,128)(2,1)S(1)}, bf16[768,8192]{1,0:T(8,128)(2,1)}, u32[]{:S(2)}) copy-start(bf16[768,8192]{1,0:T(8,128)(2,1)} %acts.21) | copy-start | bytes 37748740
  10.8 43.3 %collective-permute-start = (f16[1024,384]{1,0:T(8,128)(2,1)}, f16[1024,384]{1,0:T(8,128)(2,1)}, u32[]{:S(2)}, u32[]{:S(2)}) collective-permute-start(f16[1024,384]{1,0:T(8,128)(2,1)} %convert_element_type.204), channel_id=1, source_target_pairs={{0,8},{32,40},{64,72},{96,104},{1,9},{33,41},{65,73},{97,105},{2,1... | collective-permute-start | bytes 2359304 | tf_op jit(solution)/shard_map/ppermute | solution.py:146
  15.8 43.9 %collective-permute-start.1 = (f16[1024,384]{1,0:T(8,128)(2,1)}, f16[1024,384]{1,0:T(8,128)(2,1)}, u32[]{:S(2)}, u32[]{:S(2)}) collective-permute-start(f16[1024,384]{1,0:T(8,128)(2,1)} %convert_element_type.205), channel_id=1, source_target_pairs={{0,24},{32,56},{64,88},{96,120},{1,25},{33,57},{65,89},{97,121},{2... | collective-permute-start | bytes 2359304 | tf_op jit(solution)/shard_map/ppermute | solution.py:146
  21.0 47.3 %collective-permute-start.2 = (f16[1024,384]{1,0:T(8,128)(2,1)}, f16[1024,384]{1,0:T(8,128)(2,1)}, u32[]{:S(2)}, u32[]{:S(2)}) collective-permute-start(f16[1024,384]{1,0:T(8,128)(2,1)} %convert_element_type.206), channel_id=1, source_target_pairs={{0,2},{32,34},{64,66},{96,98},{1,3},{33,35},{65,67},{97,99},{2,4},... | collective-permute-start | bytes 2359304 | tf_op jit(solution)/shard_map/ppermute | solution.py:146
  24.6 49.5 %collective-permute-start.3 = (f16[1024,384]{1,0:T(8,128)(2,1)S(1)}, f16[1024,384]{1,0:T(8,128)(2,1)}, u32[]{:S(2)}, u32[]{:S(2)}) collective-permute-start(f16[1024,384]{1,0:T(8,128)(2,1)S(1)} %convert_element_type.207), channel_id=1, source_target_pairs={{0,6},{32,38},{64,70},{96,102},{1,7},{33,39},{65,71},{97,103},{2,0... | collective-permute-start | bytes 2359304 | tf_op jit(solution)/shard_map/ppermute | solution.py:146
  26.4 4.6 %copy-start.1 = (bf16[768,8192]{1,0:T(8,128)(2,1)S(1)}, bf16[768,8192]{1,0:T(8,128)(2,1)}, u32[]{:S(2)}) copy-start(bf16[768,8192]{1,0:T(8,128)(2,1)} %acts.21) | copy-start | bytes 37748740
  37.2 2.8 %copy-start.4 = (f32[4096,256]{1,0:T(8,128)}, f32[4096,256]{1,0:T(8,128)S(1)}, u32[]{:S(2)}) copy-start(f32[4096,256]{1,0:T(8,128)S(1)} %get-tuple-element.53) | copy-start | bytes 12582916
  40.0 48.4 %collective-permute-start.6 = (f16[4096,256]{1,0:T(8,128)(2,1)}, f16[4096,256]{1,0:T(8,128)(2,1)}, u32[]{:S(2)}, u32[]{:S(2)}) collective-permute-start(f16[4096,256]{1,0:T(8,128)(2,1)} %convert_element_type.208), channel_id=1, source_target_pairs={{0,1},{32,33},{64,65},{96,97},{1,0},{33,32},{65,64},{97,96},{2,3},... | collective-permute-start | bytes 6291464 | tf_op jit(solution)/shard_map/ppermute | solution.py:146
  45.1 4.6 %copy-start.2 = (bf16[768,8192]{1,0:T(8,128)(2,1)S(1)}, bf16[768,8192]{1,0:T(8,128)(2,1)}, u32[]{:S(2)}) copy-start(bf16[768,8192]{1,0:T(8,128)(2,1)} %acts.21) | copy-start | bytes 37748740
  49.7 6.6 %slice-start = ((s8[12582912]{0:T(1024)(128)(4,1)}), s8[4194304]{0:T(1024)(128)(4,1)S(1)}, s32[]{:S(2)}) async-start(s8[12582912]{0:T(1024)(128)(4,1)} %bitcast.178), calls=%async_computation | async-start | bytes 8388608
  49.7 6.7 %slice-start.1 = ((s8[12582912]{0:T(1024)(128)(4,1)}), s8[4194304]{0:T(1024)(128)(4,1)S(1)}, s32[]{:S(2)}) async-start(s8[12582912]{0:T(1024)(128)(4,1)} %bitcast.178), calls=%async_computation.1 | async-start | bytes 8388608
  53.0 3.3 %slice-start.2 = ((s8[12582912]{0:T(1024)(128)(4,1)}), s8[4194304]{0:T(1024)(128)(4,1)S(1)}, s32[]{:S(2)}) async-start(s8[12582912]{0:T(1024)(128)(4,1)} %bitcast.178), calls=%async_computation.2 | async-start | bytes 8388608
  56.2 37.3 %collective-permute-start.4 = (f16[2048,384]{1,0:T(8,128)(2,1)S(1)}, f16[2048,384]{1,0:T(8,128)(2,1)}, u32[]{:S(2)}, u32[]{:S(2)}) collective-permute-start(f16[2048,384]{1,0:T(8,128)(2,1)S(1)} %pad_maximum_fusion), channel_id=1, source_target_pairs={{0,8},{32,40},{64,72},{96,104},{1,9},{33,41},{65,73},{97,105},{2,1... | collective-permute-start | bytes 4718600 | tf_op jit(solution)/shard_map/ppermute | solution.py:146
  61.6 35.5 %collective-permute-start.5 = (f16[2048,384]{1,0:T(8,128)(2,1)S(1)}, f16[2048,384]{1,0:T(8,128)(2,1)}, u32[]{:S(2)}, u32[]{:S(2)}) collective-permute-start(f16[2048,384]{1,0:T(8,128)(2,1)S(1)} %pad_maximum_fusion.1), channel_id=1, source_target_pairs={{0,24},{32,56},{64,88},{96,120},{1,25},{33,57},{65,89},{97,121},{2... | collective-permute-start | bytes 4718600 | tf_op jit(solution)/shard_map/ppermute | solution.py:146
  70.2 36.0 %collective-permute-start.7 = (f16[2048,384]{1,0:T(8,128)(2,1)S(1)}, f16[2048,384]{1,0:T(8,128)(2,1)}, u32[]{:S(2)}, u32[]{:S(2)}) collective-permute-start(f16[2048,384]{1,0:T(8,128)(2,1)S(1)} %pad_maximum_fusion.2), channel_id=1, source_target_pairs={{0,2},{32,34},{64,66},{96,98},{1,3},{33,35},{65,67},{97,99},{2,4},... | collective-permute-start | bytes 4718600 | tf_op jit(solution)/shard_map/ppermute | solution.py:146
  76.0 34.7 %collective-permute-start.10 = (f16[2048,384]{1,0:T(8,128)(2,1)S(1)}, f16[2048,384]{1,0:T(8,128)(2,1)}, u32[]{:S(2)}, u32[]{:S(2)}) collective-permute-start(f16[2048,384]{1,0:T(8,128)(2,1)S(1)} %pad_maximum_fusion.3), channel_id=1, source_target_pairs={{0,6},{32,38},{64,70},{96,102},{1,7},{33,39},{65,71},{97,103},{2,0... | collective-permute-start | bytes 4718600 | tf_op jit(solution)/shard_map/ppermute | solution.py:146
  82.4 5.9 %copy-start.5 = (f32[4096,256]{1,0:T(8,128)S(1)}, f32[4096,256]{1,0:T(8,128)}, u32[]{:S(2)}) copy-start(f32[4096,256]{1,0:T(8,128)} %copy-done.4) | copy-start | bytes 12582916
  88.3 3.5 %collective-permute-start.17 = (f32[256,128]{1,0:T(8,128)S(1)}, f32[256,128]{1,0:T(8,128)S(1)}, u32[]{:S(2)}, u32[]{:S(2)}) collective-permute-start(f32[256,128]{1,0:T(8,128)S(1)} %bitcast_subtract_fusion.1), channel_id=1, source_target_pairs={{0,32},{32,0},{64,96},{96,64},{1,33},{33,1},{65,97},{97,65},{2,34}... | collective-permute-start | bytes 393224 | tf_op jit(solution)/shard_map/ppermute | solution.py:146
  91.8 29.3 %collective-permute-start.18 = (f32[256,128]{1,0:T(8,128)S(1)}, f32[256,128]{1,0:T(8,128)S(1)}, u32[]{:S(2)}, u32[]{:S(2)}) collective-permute-start(f32[256,128]{1,0:T(8,128)S(1)} %add.392), channel_id=1, source_target_pairs={{0,64},{32,96},{64,0},{96,32},{1,65},{33,97},{65,1},{97,33},{2,66}... | collective-permute-start | bytes 393224 | tf_op jit(solution)/shard_map/ppermute | solution.py:146
  110.7 10.5 %collective-permute-start.11 = (f16[256,640]{1,0:T(8,128)(2,1)S(1)}, f16[256,640]{1,0:T(8,128)(2,1)S(1)}, u32[]{:S(2)}, u32[]{:S(2)}) collective-permute-start(f16[256,640]{1,0:T(8,128)(2,1)S(1)} %get-tuple-element.60), channel_id=1, source_target_pairs={{0,6},{32,38},{64,70},{96,102},{1,7},{33,39},{65,71},{97,103},{2,0... | collective-permute-start | bytes 983048 | tf_op jit(solution)/shard_map/ppermute | solution.py:146
  114.5 8.5 %collective-permute-start.8 = (f16[256,640]{1,0:T(8,128)(2,1)S(1)}, f16[256,640]{1,0:T(8,128)(2,1)S(1)}, u32[]{:S(2)}, u32[]{:S(2)}) collective-permute-start(f16[256,640]{1,0:T(8,128)(2,1)S(1)} %get-tuple-element.57), channel_id=1, source_target_pairs={{0,2},{32,34},{64,66},{96,98},{1,3},{33,35},{65,67},{97,99},{2,4},... | collective-permute-start | bytes 983048 | tf_op jit(solution)/shard_map/ppermute | solution.py:146
  118.6 2.5 %copy-start.10 = (f32[256,1024]{1,0:T(8,128)S(1)}, f32[256,1024]{1,0:T(8,128)}, u32[]{:S(2)}) copy-start(f32[256,1024]{1,0:T(8,128)} %param.14) | copy-start | bytes 3145732
  119.0 7.6 %collective-permute-start.15 = (f16[256,640]{1,0:T(8,128)(2,1)S(1)}, f16[256,640]{1,0:T(8,128)(2,1)S(1)}, u32[]{:S(2)}, u32[]{:S(2)}) collective-permute-start(f16[256,640]{1,0:T(8,128)(2,1)S(1)} %get-tuple-element.64), channel_id=1, source_target_pairs={{0,24},{32,56},{64,88},{96,120},{1,25},{33,57},{65,89},{97,121},{2... | collective-permute-start | bytes 983048 | tf_op jit(solution)/shard_map/ppermute | solution.py:146
  119.7 8.8 %collective-permute-start.13 = (f16[256,640]{1,0:T(8,128)(2,1)S(1)}, f16[256,640]{1,0:T(8,128)(2,1)S(1)}, u32[]{:S(2)}, u32[]{:S(2)}) collective-permute-start(f16[256,640]{1,0:T(8,128)(2,1)S(1)} %get-tuple-element.62), channel_id=1, source_target_pairs={{0,8},{32,40},{64,72},{96,104},{1,9},{33,41},{65,73},{97,105},{2,1... | collective-permute-start | bytes 983048 | tf_op jit(solution)/shard_map/ppermute | solution.py:146
  121.2 1.9 %copy-start.9 = (f32[256,1024]{1,0:T(8,128)}, f32[256,1024]{1,0:T(8,128)S(1)}, u32[]{:S(2)}) copy-start(f32[256,1024]{1,0:T(8,128)S(1)} %get-tuple-element.99) | copy-start | bytes 3145732
  121.2 41.9 %copy-start.6 = (f32[256,1024]{1,0:T(8,128)}, f32[256,1024]{1,0:T(8,128)S(1)}, u32[]{:S(2)}) copy-start(f32[256,1024]{1,0:T(8,128)S(1)} %get-tuple-element.100) | copy-start | bytes 3145732
  123.3 13.5 %collective-permute-start.9 = (f16[512,640]{1,0:T(8,128)(2,1)S(1)}, f16[512,640]{1,0:T(8,128)(2,1)S(1)}, u32[]{:S(2)}, u32[]{:S(2)}) collective-permute-start(f16[512,640]{1,0:T(8,128)(2,1)S(1)} %pad_maximum_fusion.7), channel_id=1, source_target_pairs={{0,2},{32,34},{64,66},{96,98},{1,3},{33,35},{65,67},{97,99},{2,4},... | collective-permute-start | bytes 1966088 | tf_op jit(solution)/shard_map/ppermute | solution.py:146
  123.4 13.4 %collective-permute-start.12 = (f16[512,640]{1,0:T(8,128)(2,1)S(1)}, f16[512,640]{1,0:T(8,128)(2,1)S(1)}, u32[]{:S(2)}, u32[]{:S(2)}) collective-permute-start(f16[512,640]{1,0:T(8,128)(2,1)S(1)} %pad_maximum_fusion.8), channel_id=1, source_target_pairs={{0,6},{32,38},{64,70},{96,102},{1,7},{33,39},{65,71},{97,103},{2,0... | collective-permute-start | bytes 1966088 | tf_op jit(solution)/shard_map/ppermute | solution.py:146
  128.8 13.6 %collective-permute-start.14 = (f16[512,640]{1,0:T(8,128)(2,1)S(1)}, f16[512,640]{1,0:T(8,128)(2,1)S(1)}, u32[]{:S(2)}, u32[]{:S(2)}) collective-permute-start(f16[512,640]{1,0:T(8,128)(2,1)S(1)} %pad_maximum_fusion.9), channel_id=1, source_target_pairs={{0,8},{32,40},{64,72},{96,104},{1,9},{33,41},{65,73},{97,105},{2,1... | collective-permute-start | bytes 1966088 | tf_op jit(solution)/shard_map/ppermute | solution.py:146
  130.0 12.6 %collective-permute-start.16 = (f16[512,640]{1,0:T(8,128)(2,1)S(1)}, f16[512,640]{1,0:T(8,128)(2,1)S(1)}, u32[]{:S(2)}, u32[]{:S(2)}) collective-permute-start(f16[512,640]{1,0:T(8,128)(2,1)S(1)} %pad_maximum_fusion.10), channel_id=1, source_target_pairs={{0,24},{32,56},{64,88},{96,120},{1,25},{33,57},{65,89},{97,121},{2... | collective-permute-start | bytes 1966088 | tf_op jit(solution)/shard_map/ppermute | solution.py:146
  142.3 7.8 %collective-permute-start.24 = (f16[128,128]{1,0:T(8,128)(2,1)S(1)}, f16[128,128]{1,0:T(8,128)(2,1)S(1)}, u32[]{:S(2)}, u32[]{:S(2)}) collective-permute-start(f16[128,128]{1,0:T(8,128)(2,1)S(1)} %get-tuple-element.73), channel_id=1, source_target_pairs={{0,8},{32,40},{64,72},{96,104},{1,9},{33,41},{65,73},{97,105},{2,1... | collective-permute-start | bytes 98312 | tf_op jit(solution)/shard_map/ppermute | solution.py:146
  142.6 7.5 %collective-permute-start.26 = (f16[128,128]{1,0:T(8,128)(2,1)S(1)}, f16[128,128]{1,0:T(8,128)(2,1)S(1)}, u32[]{:S(2)}, u32[]{:S(2)}) collective-permute-start(f16[128,128]{1,0:T(8,128)(2,1)S(1)} %get-tuple-element.75), channel_id=1, source_target_pairs={{0,24},{32,56},{64,88},{96,120},{1,25},{33,57},{65,89},{97,121},{2... | collective-permute-start | bytes 98312 | tf_op jit(solution)/shard_map/ppermute | solution.py:146
  146.2 6.2 %collective-permute-start.22 = (f16[128,128]{1,0:T(8,128)(2,1)S(1)}, f16[128,128]{1,0:T(8,128)(2,1)S(1)}, u32[]{:S(2)}, u32[]{:S(2)}) collective-permute-start(f16[128,128]{1,0:T(8,128)(2,1)S(1)} %get-tuple-element.71), channel_id=1, source_target_pairs={{0,6},{32,38},{64,70},{96,102},{1,7},{33,39},{65,71},{97,103},{2,0... | collective-permute-start | bytes 98312 | tf_op jit(solution)/shard_map/ppermute | solution.py:146
  149.5 5.1 %collective-permute-start.20 = (f16[128,128]{1,0:T(8,128)(2,1)S(1)}, f16[128,128]{1,0:T(8,128)(2,1)S(1)}, u32[]{:S(2)}, u32[]{:S(2)}) collective-permute-start(f16[128,128]{1,0:T(8,128)(2,1)S(1)} %get-tuple-element.69), channel_id=1, source_target_pairs={{0,2},{32,34},{64,66},{96,98},{1,3},{33,35},{65,67},{97,99},{2,4},... | collective-permute-start | bytes 98312 | tf_op jit(solution)/shard_map/ppermute | solution.py:146
  149.7 11.5 %collective-permute-start.19 = (f16[256,768]{1,0:T(8,128)(2,1)S(1)}, f16[256,768]{1,0:T(8,128)(2,1)S(1)}, u32[]{:S(2)}, u32[]{:S(2)}) collective-permute-start(f16[256,768]{1,0:T(8,128)(2,1)S(1)} %fusion.12), channel_id=1, source_target_pairs={{0,1},{32,33},{64,65},{96,97},{1,0},{33,32},{65,64},{97,96},{2,3},... | collective-permute-start | bytes 1179656 | tf_op jit(solution)/shard_map/ppermute | solution.py:146
  150.2 11.2 %copy-start.7 = (f32[1,256,1024]{2,1,0:T(8,128)S(1)}, f32[1,256,1024]{2,1,0:T(8,128)}, u32[]{:S(2)}) copy-start(f32[1,256,1024]{2,1,0:T(8,128)} %param.12) | copy-start | bytes 3145732
  150.3 11.2 %copy-start.8 = (f32[1,256,1024]{2,1,0:T(8,128)S(1)}, f32[1,256,1024]{2,1,0:T(8,128)}, u32[]{:S(2)}) copy-start(f32[1,256,1024]{2,1,0:T(8,128)} %param.11) | copy-start | bytes 3145732
  150.3 6.5 %collective-permute-start.27 = (f16[256,128]{1,0:T(8,128)(2,1)S(1)}, f16[256,128]{1,0:T(8,128)(2,1)S(1)}, u32[]{:S(2)}, u32[]{:S(2)}) collective-permute-start(f16[256,128]{1,0:T(8,128)(2,1)S(1)} %pad_maximum_fusion.16), channel_id=1, source_target_pairs={{0,24},{32,56},{64,88},{96,120},{1,25},{33,57},{65,89},{97,121},{2... | collective-permute-start | bytes 196616 | tf_op jit(solution)/shard_map/ppermute | solution.py:146
  150.9 5.9 %collective-permute-start.25 = (f16[256,128]{1,0:T(8,128)(2,1)S(1)}, f16[256,128]{1,0:T(8,128)(2,1)S(1)}, u32[]{:S(2)}, u32[]{:S(2)}) collective-permute-start(f16[256,128]{1,0:T(8,128)(2,1)S(1)} %pad_maximum_fusion.15), channel_id=1, source_target_pairs={{0,8},{32,40},{64,72},{96,104},{1,9},{33,41},{65,73},{97,105},{2,1... | collective-permute-start | bytes 196616 | tf_op jit(solution)/shard_map/ppermute | solution.py:146
  154.7 4.3 %collective-permute-start.23 = (f16[256,128]{1,0:T(8,128)(2,1)S(1)}, f16[256,128]{1,0:T(8,128)(2,1)S(1)}, u32[]{:S(2)}, u32[]{:S(2)}) collective-permute-start(f16[256,128]{1,0:T(8,128)(2,1)S(1)} %pad_maximum_fusion.14), channel_id=1, source_target_pairs={{0,6},{32,38},{64,70},{96,102},{1,7},{33,39},{65,71},{97,103},{2,0... | collective-permute-start | bytes 196616 | tf_op jit(solution)/shard_map/ppermute | solution.py:146
  155.8 5.5 %collective-permute-start.21 = (f16[256,128]{1,0:T(8,128)(2,1)S(1)}, f16[256,128]{1,0:T(8,128)(2,1)S(1)}, u32[]{:S(2)}, u32[]{:S(2)}) collective-permute-start(f16[256,128]{1,0:T(8,128)(2,1)S(1)} %pad_maximum_fusion.13), channel_id=1, source_target_pairs={{0,2},{32,34},{64,66},{96,98},{1,3},{33,35},{65,67},{97,99},{2,4},... | collective-permute-start | bytes 196616 | tf_op jit(solution)/shard_map/ppermute | solution.py:146
  161.4 1.7 %copy-start.11 = (f32[1,256,1024]{2,1,0:T(8,128)S(1)}, f32[1,256,1024]{2,1,0:T(8,128)}, u32[]{:S(2)}) copy-start(f32[1,256,1024]{2,1,0:T(8,128)} %param.10) | copy-start | bytes 3145732
  161.4 1.7 %copy-start.12 = (s32[1024]{0:T(1024)S(1)}, s32[1024]{0:T(1024)}, u32[]{:S(2)}) copy-start(s32[1024]{0:T(1024)} %get-tuple-element.166) | copy-start | bytes 12292
  161.4 1.7 %copy-start.13 = (pred[1024]{0:T(1024)(128)(4,1)S(1)}, pred[1024]{0:T(1024)(128)(4,1)}, u32[]{:S(2)}) copy-start(pred[1024]{0:T(1024)(128)(4,1)} %fusion.22) | copy-start | bytes 3076
